TPU v7x, 256 devices: a whole 4x4x8 slice. The times are simulated.
256 devices in a mesh: seq: 16 (over z, x_hi), row: 8 (over y, core), col: 2 (over x_lo).
Axes of the slice: x: 4 (x_hi: 2, x_lo: 2; x = x_hi * 2 + x_lo), y: 4, z: 8, core: 2. Of those that a mesh axis runs over, the one named last changes fastest.
Arguments:
- projections: bfloat16 [3, 16384, 4096], P(None, 'seq', ('row', 'col')), may hold values from -6 to 6
- feat_filters: float32 [3, 7, 4096], P(None, None, ('row', 'col')), may hold values from -2 to 2
- long_filters: bfloat16 [256, 128], P(('row', 'col')), may hold values from -0.5 to 0.5
- out_weight: bfloat16 [4096, 8192], P('row', 'col'), may hold values from -0.09375 to 0.09375
- grad_output: bfloat16 [16384, 8192], P('seq', ('col', 'row')), may hold values from -6 to 6
Outputs:
- grad_projections: bfloat16 [3, 16384, 4096], P(None, 'seq', ('row', 'col'))
- grad_out_weight: float32 [4096, 8192], P('row', ('col', 'seq'))
- grad_long: float32 [256, 128], P(('row', 'col'))
- grad_feat: float32 [3, 7, 4096], P(None, None, ('row', 'col'))
All inputs are finite; a program needn't handle non-finite values.
Results may differ from a plain program's by a relative error of at most 0.013.
Values may be sent and summed in bfloat16 or wider, within the bound.
A program may use at most 128 MiB of HBM per device.

v0:
```python
import math

import jax
import jax.numpy as jnp
from jax import lax
from jax.sharding import PartitionSpec as P


def from_behind(value, axis, by):
    devices = lax.axis_size(axis)
    pairs = [(i, i + by) for i in range(devices) if 0 <= i + by < devices]
    return lax.ppermute(value, axis, pairs)


def tap_matrix(filters, flipped):
    group_count, filt_len = filters.shape
    if flipped:
        row_vec = jnp.concatenate(
            [
                jnp.zeros((group_count, 1), filters.dtype),
                filters[:, ::-1],
                jnp.zeros((group_count, filt_len), filters.dtype),
            ],
            1,
        )
    else:
        row_vec = jnp.concatenate(
            [filters, jnp.zeros((group_count, filt_len + 1), filters.dtype)], 1
        )
    tiled = jnp.tile(row_vec, (1, filt_len))[:, : filt_len * 2 * filt_len]
    return tiled.reshape(group_count, filt_len, 2 * filt_len)


def band_windows(extended, filt_len, group_count):
    block_count = extended.shape[0] // filt_len - 1
    blocks = extended.reshape(block_count + 1, filt_len, group_count, -1)
    return jnp.concatenate([blocks[:-1], blocks[1:]], axis=1)


def band_apply(matrix, windows):
    result = jnp.einsum("gim,bmgk->bigk", matrix, windows, preferred_element_type=jnp.float32)
    return result.reshape(result.shape[0] * result.shape[1], -1)


def on_device(projections, feat_filters, long_filters, out_weight, grad_output):
    tok_rows = projections.shape[1]
    chan_width = projections.shape[2]
    tap_count = feat_filters.shape[1]
    group_count = long_filters.shape[0]
    filt_len = long_filters.shape[1]
    grad_scale = 1.0 / math.sqrt(tok_rows * lax.axis_size("seq"))
    prev_rims = from_behind(projections[:, tok_rows - (tap_count - 1) :, :], "seq", 1)
    inputs = projections.astype(jnp.float32)
    before = jnp.concatenate([prev_rims.astype(jnp.float32), inputs], 1)
    featured = jnp.zeros(inputs.shape, jnp.float32)
    for tap_idx in range(tap_count):
        start_row = tap_count - 1 - tap_idx
        featured = (
            featured
            + feat_filters[:, tap_idx, None, :] * before[:, start_row : start_row + tok_rows]
        )
    query_feat = featured[0]
    key_feat = featured[1]
    value_feat = featured[2]
    kv_product = (key_feat * value_feat).astype(jnp.bfloat16)
    history = from_behind(kv_product[tok_rows - (filt_len - 1) :], "seq", 1)
    extended = jnp.concatenate([jnp.zeros((1, chan_width), jnp.bfloat16), history, kv_product], 0)
    kv_windows = band_windows(extended, filt_len, group_count)
    conv_out = band_apply(tap_matrix(long_filters, True), kv_windows)
    mixer_out = (query_feat * conv_out).astype(jnp.bfloat16)
    panel = lax.all_gather(grad_output, "row", axis=1, tiled=True)
    partial_mix = lax.dot_general(
        panel, out_weight, (((1,), (1,)), ((), ())), preferred_element_type=jnp.float32
    )
    grad_mix = lax.psum_scatter(partial_mix, "col", scatter_dimension=1, tiled=True).astype(
        jnp.bfloat16
    )
    paired = lax.all_gather(mixer_out, "col", axis=1, tiled=True)
    partial_weight = lax.dot_general(
        paired, panel, (((0,), (0,)), ((), ())), preferred_element_type=jnp.float32
    )
    grad_weight = (
        lax.psum_scatter(partial_weight, "seq", scatter_dimension=1, tiled=True) * grad_scale
    )
    mix_float = grad_mix.astype(jnp.float32)
    grad_conv = (mix_float * query_feat).astype(jnp.bfloat16)
    grad_query = (mix_float * conv_out).astype(jnp.bfloat16)
    conv_blocks = grad_conv.reshape(tok_rows // filt_len, filt_len, group_count, -1)
    lag_table = jnp.einsum(
        "bigk,bmgk->gim", conv_blocks, kv_windows, preferred_element_type=jnp.float32
    )
    flipped = lag_table[:, :, ::-1].reshape(group_count, -1)
    skewed = flipped[:, filt_len - 1 : filt_len - 1 + filt_len * (2 * filt_len - 1)]
    filter_part = (
        skewed.reshape(group_count, filt_len, 2 * filt_len - 1)[:, :, :filt_len].sum(axis=1)
        * grad_scale
    )
    grad_long = lax.psum(filter_part, "seq")
    future = from_behind(grad_conv[: filt_len - 1], "seq", -1)
    extended_back = jnp.concatenate(
        [grad_conv, future, jnp.zeros((1, chan_width), jnp.bfloat16)], 0
    )
    grad_kv = band_apply(
        tap_matrix(long_filters, False), band_windows(extended_back, filt_len, group_count)
    )
    grad_key = (grad_kv * value_feat).astype(jnp.bfloat16)
    grad_value = (grad_kv * key_feat).astype(jnp.bfloat16)
    stream_grads = jnp.stack([grad_query, grad_key, grad_value], 0)
    ahead = from_behind(stream_grads[:, : tap_count - 1], "seq", -1)
    grad_float = stream_grads.astype(jnp.float32)
    ahead_ext = jnp.concatenate([grad_float, ahead.astype(jnp.float32)], 1)
    back_sum = jnp.zeros(grad_float.shape, jnp.float32)
    per_tap = []
    for tap_idx in range(tap_count):
        back_sum = (
            back_sum
            + feat_filters[:, tap_idx, None, :] * ahead_ext[:, tap_idx : tap_idx + tok_rows]
        )
        start_row = tap_count - 1 - tap_idx
        per_tap.append(jnp.sum(grad_float * before[:, start_row : start_row + tok_rows], axis=1))
    grad_projections = back_sum.astype(jnp.bfloat16)
    feat_part = jnp.stack(per_tap, 1) * grad_scale
    grad_feat = lax.psum(feat_part, "seq")
    return (grad_projections, grad_weight, grad_long, grad_feat)


def solution(mesh):
    return jax.shard_map(
        on_device,
        mesh=mesh,
        in_specs=(
            P(None, "seq", ("row", "col")),
            P(None, None, ("row", "col")),
            P(("row", "col"), None),
            P("row", "col"),
            P("seq", ("col", "row")),
        ),
        out_specs=(
            P(None, "seq", ("row", "col")),
            P("row", ("col", "seq")),
            P(("row", "col"), None),
            P(None, None, ("row", "col")),
        ),
        check_vma=False,
    )
```

profile of v0, /device:TPU:32, one launch (start us, length us, event | category | flops | bytes accessed | tf_op | source)
XLA Modules:
  0.0 393.2 jit_solution(17263403850417579392)
XLA Ops:
  8.0 56.8 %all-gather.3.cloned.1.call-done = bf16[1024,4096]{1,0:T(8,128)(2,1)} async-done(((bf16[1024,512]{1,0:T(8,128)(2,1)}), bf16[1024,4096]{1,0:T(8,128)(2,1)}) %all-gather.3.cloned.1.call-update) | async-done | bytes 8388624 | tf_op jit(solution)/shard_map/all_gather | solution.py:71
  64.8 10.4 %fusion.42 = f32[1024,512]{1,0:T(8,128)} fusion(bf16[1024,4096]{1,0:T(8,128)(2,1)} %all-gather.3.cloned.1.call-done, bf16[512,4096]{1,0:T(8,128)(2,1)} %param.8), kind=kOutput, calls=%fused_computation.100 | convolution fusion | flops 4294967296 | bytes 14680064 | tf_op jit(solution)/shard_map/dot_general | solution.py:72
  75.3 4.9 %collective-permute-start = (bf16[3,6,256]{2,1,0:T(8,128)(2,1)S(1)}, bf16[3,6,256]{2,1,0:T(8,128)(2,1)S(1)}, u32[]{:S(2)}, u32[]{:S(2)}) collective-permute-start(bf16[3,6,256]{2,1,0:T(8,128)(2,1)S(1)} %slice.126), channel_id=1, source_target_pairs={{0,16},{16,32},{32,48},{48,64},{64,80},{80,96},{96,112},{112,128},... | collective-permute-start | bytes 27656 | tf_op jit(solution)/shard_map/ppermute | solution.py:12
  80.5 1.9 convert_element_type.50
  86.7 2.6 multiply_add_fusion
  90.3 3.5 collective-permute-start.1
  94.6 2.0 copy.17
  96.7 1.9 copy.45
  98.9 5.1 %concatenate.25 = bf16[1152,256]{1,0:T(8,128)(2,1)} concatenate(bf16[1,256]{1,0:T(2,128)(2,1)S(1)} %broadcast.14, bf16[127,256]{1,0:T(8,128)(2,1)S(1)} %collective-permute-done.1, bf16[1024,256]{1,0:T(8,128)(2,1)} %fusion.50), dimensions={0} | concatenate | bytes 1179648 | tf_op jit(solution)/shard_map/concatenate | solution.py:67
  105.9 2.0 copy.16
  112.5 2.5 copy.21
  115.1 2.9 multiply_convert_fusion
  118.2 26.1 %all-gather.5.cloned.1.call-done = bf16[1024,512]{1,0:T(8,128)(2,1)} async-done(((bf16[1024,256]{1,0:T(8,128)(2,1)}), bf16[1024,512]{1,0:T(8,128)(2,1)}) %all-gather.5.cloned.1.call-update) | async-done | bytes 1048592 | tf_op jit(solution)/shard_map/all_gather | solution.py:78
  144.3 11.5 %fusion.43 = f32[512,4096]{1,0:T(8,128)} fusion(bf16[1024,512]{1,0:T(8,128)(2,1)} %all-gather.5.cloned.1.call-done, bf16[1024,4096]{1,0:T(8,128)(2,1)} %all-gather.3.cloned.1.call-done), kind=kOutput, calls=%fused_computation.101 | convolution fusion | flops 4294967296 | bytes 17825792 | tf_op jit(solution)/shard_map/dot_general | solution.py:79
  157.1 3.9 tile.21
  164.4 2.0 copy.22
  166.4 4.7 %collective-permute-start.2 = (bf16[127,256]{1,0:T(8,128)(2,1)S(1)}, bf16[127,256]{1,0:T(8,128)(2,1)S(1)}, u32[]{:S(2)}, u32[]{:S(2)}) collective-permute-start(bf16[127,256]{1,0:T(8,128)(2,1)S(1)} %slice.176), channel_id=1, source_target_pairs={{16,0},{32,16},{48,32},{64,48},{80,64},{96,80},{112,96},{128,112},... | collective-permute-start | bytes 195080 | tf_op jit(solution)/shard_map/ppermute | solution.py:12
  173.1 3.1 convolution_bitcast_fusion
  176.2 17.5 %rev.7 = f32[16,128,256]{2,1,0:T(8,128)} reverse(f32[16,128,256]{2,1,0:T(8,128)} %convolution_bitcast_fusion), dimensions={2} | reverse | bytes 4194304 | tf_op jit(solution)/shard_map/rev | solution.py:92
  193.7 2.8 copy.51
  196.6 1.9 slice.190
  198.5 6.2 %reshape.55 = f32[16,128,255]{2,1,0:T(8,128)} reshape(f32[16,32640]{1,0:T(8,128)} %slice.190) | data formatting | bytes 4177920 | tf_op jit(solution)/shard_map/reshape | solution.py:95
  206.1 2.0 copy.24
  208.0 5.0 %concatenate.28 = bf16[1152,256]{1,0:T(8,128)(2,1)} concatenate(bf16[1024,256]{1,0:T(8,128)(2,1)} %get-tuple-element.24, bf16[127,256]{1,0:T(8,128)(2,1)S(1)} %collective-permute-done.2, bf16[1,256]{1,0:T(2,128)(2,1)S(1)} %broadcast.14), dimensions={0} | concatenate | bytes 1179648 | tf_op jit(solution)/shard_map/concatenate | solution.py:100
  214.9 2.0 copy.23
  221.4 2.4 reshape.53
  223.9 2.5 copy.27
  228.3 3.0 collective-permute-start.3
  231.4 3.0 fusion.12
  234.5 76.1 %all-reduce.1 = (f32[16,128]{1,0:T(8,128)}, f32[3,7,256]{2,0,1:T(4,128)S(1)}) all-reduce(f32[16,128]{1,0:T(8,128)S(1)} %broadcast_multiply_fusion.2, f32[3,7,256]{2,0,1:T(4,128)S(1)} %broadcast_multiply_fusion.1), channel_id=1, replica_groups=mesh['seq'=16,'row'=8,'col'=2] {'seq'}, use_global_device_ids=true, to_apply=%region_3.0 | all-reduce | flops 7424 | bytes 59392 | tf_op jit(solution)/shard_map/psum | solution.py:98
  311.2 6.9 %fusion.6 = bf16[3,1024,256]{2,1,0:T(8,128)(2,1)} fusion(f32[3,6,256]{2,1,0:T(8,128)S(1)} %convert_element_type.60, f32[3,1024,256]{2,1,0:T(8,128)S(1)} %get-tuple-element.26, f32[3,256]{1,0:T(4,128)S(1)} %get-tuple-element.35, f32[3,256]{1,0:T(4,128)S(1)} %get-tuple-element.36, f32[3,256]{1,0:T(4,128)S(1)} %get-tuple-element.37, ...), kind=kLoop, calls=%fused_computation.24 | loop fusion | flops 18087936 | bytes 6331392 | tf_op jit(solution)/shard_map/convert_element_type | solution.py:121
  318.1 66.7 %reduce-scatter.5.cloned.1.call-done = f32[512,256]{1,0:T(8,128)} async-done(((f32[512,4096]{1,0:T(8,128)}), f32[512,256]{1,0:T(8,128)}) %reduce-scatter.5.cloned.1.call-update) | async-done | bytes 524304 | tf_op jit(solution)/shard_map/reduce_scatter | solution.py:83
  (93 shorter events, 32.7 us)
Async XLA Ops:
  7.2 57.6 %all-gather.3.cloned.1.call-start = ((), (), s32[]{:S(2)}) async-start(), calls=%async_computation.2 | async-start | bytes 9437184 | tf_op jit(solution)/shard_map/all_gather | solution.py:71
  7.9 67.4 %copy-start.6 = (bf16[3,1024,256]{2,1,0:T(8,128)(2,1)S(1)}, bf16[3,1024,256]{2,1,0:T(8,128)(2,1)}, u32[]{:S(2)}) copy-start(bf16[3,1024,256]{2,1,0:T(8,128)(2,1)} %param.5) | copy-start | bytes 4718596
  7.9 72.3 %copy-start.12 = (bf16[16,128]{1,0:T(8,128)(2,1)S(1)}, bf16[16,128]{1,0:T(8,128)(2,1)}, u32[]{:S(2)}) copy-start(bf16[16,128]{1,0:T(8,128)(2,1)} %param.7) | copy-start | bytes 12292
  7.9 72.5 %copy-start.11 = (f32[3,7,256]{2,1,0:T(8,128)S(1)}, f32[3,7,256]{2,1,0:T(8,128)}, u32[]{:S(2)}) copy-start(f32[3,7,256]{2,1,0:T(8,128)} %param.6) | copy-start | bytes 64516
  7.9 107.1 %reduce-scatter.3.cloned.1.call-start = ((), (), s32[]{:S(2)}) async-start(), calls=%async_computation.3 | async-start | bytes 3145728 | tf_op jit(solution)/shard_map/reduce_scatter | solution.py:75
  75.2 69.1 %all-gather.5.cloned.1.call-start = ((), (), s32[]{:S(2)}) async-start(), calls=%async_computation.4 | async-start | bytes 1572864 | tf_op jit(solution)/shard_map/all_gather | solution.py:78
  75.3 10.4 %collective-permute-start = (bf16[3,6,256]{2,1,0:T(8,128)(2,1)S(1)}, bf16[3,6,256]{2,1,0:T(8,128)(2,1)S(1)}, u32[]{:S(2)}, u32[]{:S(2)}) collective-permute-start(bf16[3,6,256]{2,1,0:T(8,128)(2,1)S(1)} %slice.126), channel_id=1, source_target_pairs={{0,16},{16,32},{32,48},{48,64},{64,80},{80,96},{96,112},{112,128},... | collective-permute-start | bytes 27656 | tf_op jit(solution)/shard_map/ppermute | solution.py:12
  84.5 2.3 copy-start
  89.4 0.8 copy-start.10
  90.3 8.6 %collective-permute-start.1 = (bf16[127,256]{1,0:T(8,128)(2,1)S(1)}, bf16[127,256]{1,0:T(8,128)(2,1)S(1)}, u32[]{:S(2)}, u32[]{:S(2)}) collective-permute-start(bf16[127,256]{1,0:T(8,128)(2,1)S(1)} %slice_bitcast_fusion.1), channel_id=1, source_target_pairs={{0,16},{16,32},{32,48},{48,64},{64,80},{80,96},{96,112},{112,128},... | collective-permute-start | bytes 195080 | tf_op jit(solution)/shard_map/ppermute | solution.py:12
  107.9 2.6 copy-start.9
  110.6 2.0 copy-start.5
  118.0 266.8 %reduce-scatter.5.cloned.1.call-start = ((), (), s32[]{:S(2)}) async-start(), calls=%async_computation.5 | async-start | bytes 8912896 | tf_op jit(solution)/shard_map/reduce_scatter | solution.py:83
  166.4 41.6 %collective-permute-start.2 = (bf16[127,256]{1,0:T(8,128)(2,1)S(1)}, bf16[127,256]{1,0:T(8,128)(2,1)S(1)}, u32[]{:S(2)}, u32[]{:S(2)}) collective-permute-start(bf16[127,256]{1,0:T(8,128)(2,1)S(1)} %slice.176), channel_id=1, source_target_pairs={{16,0},{32,16},{48,32},{64,48},{80,64},{96,80},{112,96},{128,112},... | collective-permute-start | bytes 195080 | tf_op jit(solution)/shard_map/ppermute | solution.py:12
  172.3 0.8 copy-start.8
  226.4 1.5 copy-start.2
  227.9 3.4 copy-start.3
  227.9 3.4 copy-start.4
  228.0 3.4 copy-start.1
  228.0 3.4 copy-start.7
  228.3 82.9 %collective-permute-start.3 = (bf16[3,6,256]{2,1,0:T(8,128)(2,1)S(1)}, bf16[3,6,256]{2,1,0:T(8,128)(2,1)S(1)}, u32[]{:S(2)}, u32[]{:S(2)}) collective-permute-start(bf16[3,6,256]{2,1,0:T(8,128)(2,1)S(1)} %slice.179), channel_id=1, source_target_pairs={{16,0},{32,16},{48,32},{64,48},{80,64},{96,80},{112,96},{128,112},... | collective-permute-start | bytes 27656 | tf_op jit(solution)/shard_map/ppermute | solution.py:12
Sparse Core Ops, SparseCore 0:
  9.8 54.8 all-gather.2
  75.4 38.4 reduce-scatter.2
  118.1 26.1 all-gather.4
  156.0 228.7 reduce-scatter.4
where the time goes:
time: 397 us; the launch traced here: 393 us
  waiting for transfers between devices  151 us (38%)
  local copies, waits for them, and re-layouts  85.1 us (21%)
  blocking collectives  76.1 us (19%)
  matrix products  27.4 us (7%)
  other arithmetic  23.5 us (6%)
  starting transfers between devices  16.4 us (4%)
  between operations  14.2 us (4%)
    psum x1, blocking collectives, on_device(): grad_long = lax.psum(filter_part, 'seq')  76.1 us
    reduce_scatter x1, waiting for transfers between devices, on_device(): lax.psum_scatter(partial_weight, 'seq', scatter_dimension=1, tiled=True)  66.7 us
    all_gather x1, waiting for transfers between devices, on_device(): panel = lax.all_gather(grad_output, 'row', axis=1, tiled=True)  56.8 us
    all_gather x1, waiting for transfers between devices, on_device(): paired = lax.all_gather(mixer_out, 'col', axis=1, tiled=True)  26.1 us
    rev x1, local copies, waits for them, and re-layouts, on_device(): flipped = lag_table[:, :, ::-1].reshape(group_count, -1)  17.5 us
    ppermute x4, starting transfers between devices, from_behind(): return lax.ppermute(value, axis, pairs)  16.1 us
    unnamed x46, local copies, waits for them, and re-layouts  15.2 us
    dot_general x1, matrix products, on_device(): lax.dot_general(paired, panel, (((0,), (0,)), ((), ())), preferred_elemen...  11.5 us
  transfers between devices with their start and end apart: 8, of which 4 were waited for; matrix products, arithmetic and copies ran while one was open for 27% of the time, Pallas kernels for 0%

commit v1 on v0

v1 whole, which is shorter than its diff:
```python
import functools
import math

import jax
import jax.numpy as jnp
from jax import lax
from jax.experimental import pallas as pl
from jax.experimental.pallas import tpu as pltpu
from jax.sharding import PartitionSpec as P

MESH = pl.DeviceIdType.MESH
F32 = jnp.float32
BF16 = jnp.bfloat16
NN = (((1,), (0,)), ((), ()))
NT = (((1,), (1,)), ((), ()))
TN = (((0,), (0,)), ((), ()))
Z = 8
Y = 4
TOK = 1024
CH = 256
LANES = 128
BLOCKS = TOK // LANES
GROUPS = 16
GS = 16
TAPS = 7
PARTS = 4
RIM = 16
ORDER = (0, 2, 1, 3)
UNITS = 2 * PARTS
COPIES = 160


def dot(a, b, dims):
    return lax.dot_general(a, b, dims, preferred_element_type=F32)


def kernel(
    grad_scale,
    proj,
    ff,
    lf,
    w_hbm,
    go_hbm,
    gp_out,
    gw_out,
    gl_out,
    gf_out,
    projx,
    feat,
    kvx,
    conv,
    mix,
    toep,
    wv,
    gath,
    pm,
    part,
    rsbuf,
    gwacc,
    xs,
    xr,
    gms,
    gmr,
    gcx,
    gback,
    gtok,
    rim_in,
    rim_out,
    rim_back,
    red,
    redx,
    redz,
    ssem,
    rsem,
    lsem,
):
    s = lax.axis_index("seq")
    r = lax.axis_index("row")
    q = lax.axis_index("col")
    seqs = 2 * Z
    z, xh = s // 2, s % 2
    y, core = r // 2, r % 2

    def at_z(k):
        return (((z + k) % Z) * 2 + xh, r, q)

    def at_y(k):
        return (s, ((y + k) % Y) * 2 + core, q)

    def row_y(k, c):
        return ((y + k) % Y) * 2 + c

    sibling = (s, y * 2 + 1 - core, q)
    across = (z * 2 + 1 - xh, r, q)
    column = (s, r, 1 - q)
    after = ((s + 1) % seqs, r, q)
    behind = ((s + seqs - 1) % seqs, r, q)
    diagonal = (((z + 2 * xh - 1 + Z) % Z) * 2 + 1 - xh, r, q)

    used = [0]
    sent = []

    def push(src, dst, device):
        idx = used[0]
        used[0] += 1
        copy = pltpu.make_async_remote_copy(
            src_ref=src,
            dst_ref=dst,
            send_sem=ssem.at[idx],
            recv_sem=rsem.at[idx],
            device_id=device,
            device_id_type=MESH,
        )
        copy.start()
        sent.append(copy)
        return idx

    def arrived(idx, ref):
        pltpu.make_async_remote_copy(
            src_ref=ref,
            dst_ref=ref,
            send_sem=ssem.at[idx],
            recv_sem=rsem.at[idx],
            device_id=sibling,
            device_id_type=MESH,
        ).wait_recv()

    w_loads = []
    for p in range(PARTS):
        for blk in range(2 * Y):
            copy = pltpu.make_async_copy(
                w_hbm.at[:, pl.ds(512 * blk + LANES * ORDER[p], LANES)],
                wv.at[p, :, pl.ds(LANES * blk, LANES)],
                lsem.at[p * 9 + blk],
            )
            copy.start()
            w_loads.append(copy)
    own_loads = []
    for p in range(PARTS):
        copy = pltpu.make_async_copy(
            go_hbm.at[:, pl.ds(LANES * ORDER[p], LANES)], gath.at[p, r], lsem.at[p * 9 + 8]
        )
        copy.start()
        own_loads.append(copy)

    barrier = pltpu.get_barrier_semaphore()
    partners = [at_z(k) for k in range(1, Z)] + [at_y(1), at_y(-1 + Y), sibling, across, column, diagonal]
    for device in partners:
        pl.semaphore_signal(barrier, inc=1, device_id=device, device_id_type=MESH)
    pl.semaphore_wait(barrier, len(partners))

    ids = {}

    def gather_direct(p):
        src = go_hbm.at[:, pl.ds(LANES * ORDER[p], LANES)]
        ids[p, 0] = push(src, gath.at[p, r], at_y(1))
        ids[p, 1] = push(src, gath.at[p, r], at_y(Y - 1))
        ids[p, 2] = push(src, gath.at[p, r], sibling)

    half = pl.ds(0, TOK // 2), pl.ds(TOK // 2, TOK // 2)

    def gather_forward(p):
        low, high = row_y(Y - 1, core), row_y(1, core)
        arrived(ids[p, 0], gath.at[p, low])
        ids[p, 3] = push(gath.at[p, low, half[0]], gath.at[p, low, half[0]], at_y(1))
        ids[p, 5] = push(gath.at[p, low], gath.at[p, low], sibling)
        arrived(ids[p, 1], gath.at[p, high])
        ids[p, 4] = push(gath.at[p, high, half[1]], gath.at[p, high, half[1]], at_y(Y - 1))
        ids[p, 6] = push(gath.at[p, high], gath.at[p, high], sibling)

    def gather_finish(p):
        far = row_y(2, core)
        arrived(ids[p, 3], gath.at[p, far, half[0]])
        arrived(ids[p, 4], gath.at[p, far, half[1]])
        ids[p, 7] = push(gath.at[p, far], gath.at[p, far], sibling)
        own_loads[p].wait()
        for idx, k in ((2, 0), (5, Y - 1), (6, 1), (7, 2)):
            arrived(ids[p, idx], gath.at[p, row_y(k, 1 - core)])

    gather_direct(0)
    rim_id = push(proj.at[:, pl.ds(TOK - RIM, RIM), :], rim_in, after)
    gather_direct(1)

    taps32 = lf[...].astype(F32)
    base = jnp.broadcast_to(taps32[:, None, :], (GROUPS, 8, LANES)).reshape(GROUPS * 8, LANES)
    sub = lax.broadcasted_iota(jnp.int32, (GROUPS * 8, LANES), 0) % 8
    for bit in (1, 2, 4):
        base = jnp.where((sub // bit) % 2 == 1, pltpu.roll(base, bit, 1), base)
    lane3 = lax.broadcasted_iota(jnp.int32, (GROUPS, 16, LANES), 2)
    sub3 = lax.broadcasted_iota(jnp.int32, (GROUPS, 16, LANES), 1)
    for a in range(LANES // 16):
        low = pltpu.roll(base, 16 * a, 1) if a else base
        high = pltpu.roll(base, 16 * a + 8, 1)
        both = jnp.concatenate(
            [low.reshape(GROUPS, 8, LANES), high.reshape(GROUPS, 8, LANES)], axis=1
        )
        later = lane3 < sub3 + 16 * a
        toep[:, pl.ds(16 * a, 16), :] = jnp.where(later, both, 0.0).astype(BF16)
        toep[:, pl.ds(LANES + 16 * a, 16), :] = jnp.where(later, 0.0, both).astype(BF16)

    def widen(b, carry):
        rows = pl.ds(pl.multiple_of(b * LANES, LANES), LANES)
        dest = pl.ds(pl.multiple_of(b * LANES + RIM, RIM), LANES)
        for a in range(3):
            block = proj[a, rows, :].astype(F32)
            for h in range(2):
                projx[a, h, dest, :] = block[:, LANES * h : LANES * h + LANES]
        return carry

    lax.fori_loop(0, BLOCKS, widen, 0)

    def featurize(b):
        start = b * LANES + RIM
        cols = pl.ds(b * LANES if isinstance(b, int) else pl.multiple_of(b * LANES, LANES), LANES)
        for h in range(2):
            chans = pl.ds(LANES * h, LANES)
            turned = []
            for a in range(3):
                total = ff[a, pl.ds(0, 1), chans] * projx[a, h, pl.ds(start, LANES), :]
                for i in range(1, TAPS):
                    total = total + ff[a, pl.ds(i, 1), chans] * projx[a, h, pl.ds(start - i, LANES), :]
                total = total.T
                feat[a, chans, cols] = total
                turned.append(total)
            product = (turned[1] * turned[2]).astype(BF16)
            ahead = b * LANES + LANES
            kvx[chans, pl.ds(ahead if isinstance(b, int) else pl.multiple_of(ahead, LANES), LANES)] = product

    featurize(BLOCKS - 1)
    hist_id = push(kvx.at[:, pl.ds(TOK, LANES)], kvx.at[:, pl.ds(0, LANES)], after)

    def feat_loop(b, carry):
        featurize(b)
        return carry

    lax.fori_loop(1, BLOCKS - 1, feat_loop, 0)
    arrived(rim_id, rim_in)
    for a in range(3):
        before = jnp.where(s == 0, 0.0, rim_in[a].astype(F32))
        for h in range(2):
            projx[a, h, pl.ds(0, RIM), :] = before[:, LANES * h : LANES * h + LANES]
    featurize(0)

    gather_forward(0)
    gather_direct(2)

    arrived(hist_id, kvx.at[:, pl.ds(0, LANES)])
    past = kvx[:, pl.ds(0, LANES)]
    kvx[:, pl.ds(0, LANES)] = jnp.where(s == 0, jnp.zeros_like(past), past)

    def stacked(ref, rows, first):
        return jnp.concatenate(
            [ref[rows, pl.ds(LANES * (b + first), LANES)] for b in range(BLOCKS)], axis=0
        )

    def convolve(g, carry):
        rows = pl.ds(pl.multiple_of(g * GS, GS), GS)
        windows = jnp.concatenate([stacked(kvx, rows, 0), stacked(kvx, rows, 1)], axis=1)
        result = dot(windows, toep[g], NN)
        for b in range(BLOCKS):
            cols = pl.ds(LANES * b, LANES)
            piece = result[GS * b : GS * b + GS]
            conv[rows, cols] = piece
            mix[q, rows, cols] = (feat[0, rows, cols] * piece).astype(BF16)
        return carry

    mix_ids = []
    for h in range(2):
        lax.fori_loop(h * GROUPS // 2, (h + 1) * GROUPS // 2, convolve, 0)
        chans = pl.ds(LANES * h, LANES)
        mix_ids.append((push(mix.at[q, chans], mix.at[q, chans], column), chans))

    rs = {}
    top, bottom = pl.ds(0, CH // 2), pl.ds(CH // 2, CH // 2)

    def side(n):
        return q if n % 2 == 0 else 1 - q

    def partial_weight(n):
        p, hh = n // 2, side(n)

        def pair(i, carry):
            rhs = jnp.concatenate([gath[p, 2 * i], gath[p, 2 * i + 1]], axis=1)
            result = dot(mix[hh], rhs, NN).astype(BF16)
            part[n, 2 * i] = result[:, :LANES]
            part[n, 2 * i + 1] = result[:, LANES:]
            return carry

        lax.fori_loop(0, Y, pair, 0)

    def hop(n, k):
        ahead, back = (z + k) % Z, (z - k + Z) % Z
        if k == 4:
            rs[n, 0, 0] = push(part.at[n, ahead, top], rsbuf.at[n, 0, 0, top], at_z(1))
            rs[n, 1, 0] = push(part.at[n, ahead, bottom], rsbuf.at[n, 1, 0, bottom], at_z(Z - 1))
            return
        step = 3 - k
        for way, dest, span, there in ((0, ahead, top, 1), (1, back, bottom, Z - 1)):
            rows = span if k == 3 else pl.ds(0, CH)
            arrived(rs[n, way, step], rsbuf.at[n, way, step, rows])
            part[n, dest, rows] = (
                part[n, dest, rows].astype(F32) + rsbuf[n, way, step, rows].astype(F32)
            ).astype(BF16)
            rs[n, way, step + 1] = push(part.at[n, dest], rsbuf.at[n, way, step + 1], at_z(there))

    def final_sum(n):
        for way in range(2):
            arrived(rs[n, way, 3], rsbuf.at[n, way, 3])
        gwacc[n // 2, side(n)] = (
            part[n, z].astype(F32) + rsbuf[n, 0, 3].astype(F32) + rsbuf[n, 1, 3].astype(F32)
        )

    xids = []

    def exchange(pair):
        xs[pair] = gwacc[2 * pair + 1 - xh].astype(BF16)
        xids.append(push(xs.at[pair], xr.at[pair], across))

    def tick(t):
        if t < UNITS:
            partial_weight(t)
            hop(t, 4)
        for lag in (1, 2, 3):
            if 0 <= t - lag < UNITS:
                hop(t - lag, 4 - lag)
        if 0 <= t - 4 < UNITS:
            final_sum(t - 4)
            if t - 4 == 3:
                exchange(0)
            if t - 4 == 7:
                exchange(1)

    def mix_tile(p, hh, j):
        trows = pl.ds(pl.multiple_of(j * CH, CH), CH)
        crows = pl.ds(pl.multiple_of(hh * CH, CH), CH)
        rhs = jnp.concatenate([gath[p, i, trows, :] for i in range(2 * Y)], axis=1)
        return dot(wv[p, crows, :], rhs, NT)

    def partial_mix(p):
        def tile(j, carry):
            for hh in range(2):
                value = mix_tile(p, hh, j)
                if p == 0:
                    pm[j, hh] = value
                else:
                    pm[j, hh] += value
            return carry

        lax.fori_loop(0, TOK // CH, tile, 0)

    gather_forward(1)
    gather_direct(3)
    for copy in w_loads:
        copy.wait()
    for p in range(PARTS - 1):
        gather_finish(p)
        tick(2 * p)
        gather_forward(p + 2) if p + 2 < PARTS else None
        partial_mix(p)
        if p == 0:
            for idx, chans in mix_ids:
                arrived(idx, mix.at[1 - q, chans])
        tick(2 * p + 1)

    last = PARTS - 1
    gather_finish(last)
    gm_ids = []
    for j in range(TOK // CH):
        gms[j] = (pm[j, 1 - q] + mix_tile(last, 1 - q, j)).astype(BF16)
        gm_ids.append(push(gms.at[j], gmr.at[j], column))
    tick(6)
    for j in range(TOK // CH):
        pm[j, q] += mix_tile(last, q, j)
    tick(7)

    for j in range(TOK // CH):
        arrived(gm_ids[j], gmr.at[j])
        cols = pl.ds(CH * j, CH)
        cot = (pm[j, q] + gmr[j].astype(F32)).astype(BF16).astype(F32)
        gcx[:, cols] = (cot * feat[0, :, cols]).astype(BF16)
        gback[0, :, cols] = (cot * conv[:, cols]).astype(BF16).astype(F32)
        if j == 0:
            future_id = push(gcx.at[:, pl.ds(0, LANES)], gcx.at[:, pl.ds(TOK, LANES)], behind)
    tick(8)

    lane = lax.broadcasted_iota(jnp.int32, (LANES, LANES), 1)
    row = lax.broadcasted_iota(jnp.int32, (LANES, LANES), 0)

    def lags(g, carry):
        rows = pl.ds(pl.multiple_of(g * GS, GS), GS)
        cot = stacked(gcx, rows, 0)
        upper = dot(stacked(kvx, rows, 0), cot, TN)
        lower = dot(stacked(kvx, rows, 1), cot, TN)
        table = jnp.where(lane < row, upper, lower)
        height = LANES // 2
        while height >= 8:
            table = table[:height] + pltpu.roll(table[height:], LANES - height, 1)
            height //= 2
        redx[1, pl.ds(pl.multiple_of(g * 8, 8), 8), :] = table
        return carry

    lax.fori_loop(0, GROUPS, lags, 0)
    table = redx[1]
    for bit in (1, 2, 4):
        table = jnp.where((sub // bit) % 2 == 1, pltpu.roll(table, LANES - bit, 1), table)
    red[pl.ds(0, GROUPS), :] = jnp.sum(table.reshape(GROUPS, 8, LANES), axis=1)
    tick(9)

    arrived(future_id, gcx.at[:, pl.ds(TOK, LANES)])
    coming = gcx[:, pl.ds(TOK, LANES)]
    gcx[:, pl.ds(TOK, LANES)] = jnp.where(s == seqs - 1, jnp.zeros_like(coming), coming)

    def deconvolve(g, carry):
        rows = pl.ds(pl.multiple_of(g * GS, GS), GS)
        windows = jnp.concatenate([stacked(gcx, rows, 0), stacked(gcx, rows, 1)], axis=1)
        band = jnp.concatenate([toep[g, pl.ds(LANES, LANES), :], toep[g, pl.ds(0, LANES), :]], axis=1)
        result = dot(windows, band, NT)
        for b in range(BLOCKS):
            cols = pl.ds(LANES * b, LANES)
            piece = result[GS * b : GS * b + GS]
            gback[1, rows, cols] = (piece * feat[2, rows, cols]).astype(BF16).astype(F32)
            gback[2, rows, cols] = (piece * feat[1, rows, cols]).astype(BF16).astype(F32)
        return carry

    lax.fori_loop(0, GROUPS, deconvolve, 0)
    tick(10)

    def turn(b, carry):
        cols = pl.ds(pl.multiple_of(b * LANES, LANES), LANES)
        for a in range(3):
            for h in range(2):
                gtok[a, h, cols, :] = gback[a, pl.ds(LANES * h, LANES), cols].T
        return carry

    lax.fori_loop(0, BLOCKS, turn, 0)
    for a in range(3):
        for h in range(2):
            rim_out[a, :, pl.ds(LANES * h, LANES)] = gtok[a, h, pl.ds(0, RIM), :].astype(BF16)
    back_id = push(rim_out, rim_back, behind)
    tick(11)

    span = 64

    def tap_sums(a, h):
        def body(b, sums):
            start = pl.multiple_of(b * span, span)
            grad = gtok[a, h, pl.ds(start, span), :]
            out = []
            for i in range(TAPS):
                value = grad * projx[a, h, pl.ds(start + RIM - i, span), :]
                out.append(sums[i] + jnp.sum(value.reshape(span // 8, 8, LANES), axis=0))
            return tuple(out)

        sums = lax.fori_loop(0, TOK // span, body, tuple(jnp.zeros((8, LANES), F32) for _ in range(TAPS)))
        rows = [jnp.sum(x, axis=0, keepdims=True) for x in sums] + [jnp.zeros((1, LANES), F32)]
        red[pl.ds(GROUPS + 8 * (2 * a + h), 8), :] = jnp.concatenate(rows, axis=0)

    for a in range(3):
        for h in range(2):
            tap_sums(a, h)
    width = GROUPS + 48
    red_id = push(red, redx.at[0, pl.ds(0, width), :], across)

    def taps_back(a, h, first, count):
        chans = pl.ds(LANES * h, LANES)

        def body(b, carry):
            start = pl.multiple_of(b * span, span)
            total = ff[a, pl.ds(0, 1), chans] * gtok[a, h, pl.ds(start, span), :]
            for i in range(1, TAPS):
                total = total + ff[a, pl.ds(i, 1), chans] * gtok[a, h, pl.ds(start + i, span), :]
            gp_out[a, pl.ds(start, span), chans] = total.astype(BF16)
            return carry

        lax.fori_loop(first, first + count, body, 0)

    for h in range(2):
        taps_back(0, h, 0, TOK // span - 1)
    arrived(red_id, redx.at[0, pl.ds(0, width), :])
    redz[0] = red[...] + redx[0, pl.ds(0, width), :]
    z_ids = [push(redz.at[0], redz.at[k], at_z(k)) for k in range(1, Z)]
    for a in (1, 2):
        for h in range(2):
            taps_back(a, h, 0, TOK // span - 1)
    arrived(back_id, rim_back)
    for a in range(3):
        rest = jnp.where(s == seqs - 1, 0.0, rim_back[a].astype(F32))
        for h in range(2):
            gtok[a, h, pl.ds(TOK, RIM), :] = rest[:, LANES * h : LANES * h + LANES]
            taps_back(a, h, TOK // span - 1, 1)

    for pair in range(2):
        arrived(xids[pair], xr.at[pair])
        for hh in range(2):
            gw_out[pl.ds(CH * hh, CH), pl.ds(LANES * pair, LANES)] = (
                gwacc[2 * pair + xh, hh] + xr[pair, hh].astype(F32)
            ) * grad_scale

    for k in range(1, Z):
        arrived(z_ids[k - 1], redz.at[k])
    total = redz[0]
    for k in range(1, Z):
        total = total + redz[k]
    total = total * grad_scale
    gl_out[...] = total[:GROUPS]
    for a in range(3):
        for h in range(2):
            at = GROUPS + 8 * (2 * a + h)
            gf_out[a, :, pl.ds(LANES * h, LANES)] = total[at : at + TAPS]
    for copy in sent:
        copy.wait_send()


def on_device(projections, feat_filters, long_filters, out_weight, grad_output):
    grad_scale = 1.0 / math.sqrt(TOK * 2 * Z)
    vmem = pl.BlockSpec(memory_space=pltpu.VMEM)
    anywhere = pl.BlockSpec(memory_space=pl.ANY)
    return pl.pallas_call(
        functools.partial(kernel, grad_scale),
        out_shape=(
            jax.ShapeDtypeStruct((3, TOK, CH), BF16),
            jax.ShapeDtypeStruct((2 * CH, 2 * LANES), F32),
            jax.ShapeDtypeStruct((GROUPS, LANES), F32),
            jax.ShapeDtypeStruct((3, TAPS, CH), F32),
        ),
        in_specs=[vmem, vmem, vmem, anywhere, anywhere],
        out_specs=(vmem, vmem, vmem, vmem),
        scratch_shapes=[
            pltpu.VMEM((3, 2, TOK + RIM, LANES), F32),
            pltpu.VMEM((3, CH, TOK), F32),
            pltpu.VMEM((CH, TOK + LANES), BF16),
            pltpu.VMEM((CH, TOK), F32),
            pltpu.VMEM((2, CH, TOK), BF16),
            pltpu.VMEM((GROUPS, 2 * LANES, LANES), BF16),
            pltpu.VMEM((PARTS, 2 * CH, 2 * Y * LANES), BF16),
            pltpu.VMEM((PARTS, 2 * Y, TOK, LANES), BF16),
            pltpu.VMEM((TOK // CH, 2, CH, CH), F32),
            pltpu.VMEM((UNITS, Z, CH, LANES), BF16),
            pltpu.VMEM((UNITS, 2, 4, CH, LANES), BF16),
            pltpu.VMEM((PARTS, 2, CH, LANES), F32),
            pltpu.VMEM((2, 2, CH, LANES), BF16),
            pltpu.VMEM((2, 2, CH, LANES), BF16),
            pltpu.VMEM((TOK // CH, CH, CH), BF16),
            pltpu.VMEM((TOK // CH, CH, CH), BF16),
            pltpu.VMEM((CH, TOK + LANES), BF16),
            pltpu.VMEM((3, CH, TOK), F32),
            pltpu.VMEM((3, 2, TOK + RIM, LANES), F32),
            pltpu.VMEM((3, RIM, CH), BF16),
            pltpu.VMEM((3, RIM, CH), BF16),
            pltpu.VMEM((3, RIM, CH), BF16),
            pltpu.VMEM((GROUPS + 48, LANES), F32),
            pltpu.VMEM((2, 8 * GROUPS, LANES), F32),
            pltpu.VMEM((Z, GROUPS + 48, LANES), F32),
            pltpu.SemaphoreType.DMA((COPIES,)),
            pltpu.SemaphoreType.DMA((COPIES,)),
            pltpu.SemaphoreType.DMA((9 * PARTS,)),
        ],
        compiler_params=pltpu.CompilerParams(
            collective_id=0, has_side_effects=True, vmem_limit_bytes=60 * 1024 * 1024
        ),
        cost_estimate=pl.CostEstimate(
            flops=9_000_000_000, bytes_accessed=20_000_000, transcendentals=0
        ),
    )(projections, feat_filters, long_filters, out_weight, grad_output)


def solution(mesh):
    return jax.shard_map(
        on_device,
        mesh=mesh,
        in_specs=(
            P(None, "seq", ("row", "col")),
            P(None, None, ("row", "col")),
            P(("row", "col"), None),
            P("row", "col"),
            P("seq", ("col", "row")),
        ),
        out_specs=(
            P(None, "seq", ("row", "col")),
            P("row", ("col", "seq")),
            P(("row", "col"), None),
            P(None, None, ("row", "col")),
        ),
        check_vma=False,
    )
```

time: 397 us -> 112 us (0.28)
  waiting for transfers between devices: 151 us -> 0 us
  Pallas kernels: 0 us -> 106 us
  local copies, waits for them, and re-layouts: 85.1 us -> 4.72 us
  blocking collectives: 76.1 us -> 0 us
  matrix products: 27.4 us -> 0 us
  other arithmetic: 23.5 us -> 0 us
  starting transfers between devices: 16.4 us -> 0 us
  between operations: 14.2 us -> 0.67 us
    pallas_call x0 -> x1, Pallas kernels: none -> 106 us  [on_device(): pl.pallas_call(functools.partial(kernel, grad_scale), out_shape=(jax.Shap...]
    all_gather x2 -> x0, waiting for transfers between devices: 82.9 us -> none  [the longest x1 56.8 us: on_device(): panel = lax.all_gather(grad_output, 'row', axis=1, tiled=True)]
    psum x1 -> x0, blocking collectives: 76.1 us -> none  [on_device(): grad_long = lax.psum(filter_part, 'seq')]
    reduce_scatter x2 -> x0, waiting for transfers between devices: 66.7 us -> none  [the longest x1 66.7 us: on_device(): lax.psum_scatter(partial_weight, 'seq', scatter_dimension=1, tiled=True)]
    dot_general x5 -> x0, matrix products: 27.4 us -> none  [the longest x1 11.5 us: on_device(): lax.dot_general(paired, panel, (((0,), (0,)), ((), ())), preferred_elemen...]
    rev x2 -> x0, local copies, waits for them, and re-layouts: 17.6 us -> none  [the longest x1 17.5 us: on_device(): flipped = lag_table[:, :, ::-1].reshape(group_count, -1)]
    ppermute x4 -> x0, starting transfers between devices: 16.1 us -> none  [from_behind(): return lax.ppermute(value, axis, pairs)]
    convert_element_type x9 -> x0, other arithmetic: 14.5 us -> none  [the longest x1 6.87 us: on_device(): grad_projections = back_sum.astype(jnp.bfloat16)]
  transfers between devices with their start and end apart: 8 -> 0, of which waited for: 4 -> 0; matrix products, arithmetic and copies ran while one was open for 27% -> 0% of each run, Pallas kernels for 0% -> 0%
where the time goes in v1:
time: 112 us
  Pallas kernels  106 us (95%)
  local copies, waits for them, and re-layouts  4.72 us (4%)
    pallas_call x1, Pallas kernels, on_device(): pl.pallas_call(functools.partial(kernel, grad_scale), out_shape=(jax.Shap...  106 us
    unnamed x10, local copies, waits for them, and re-layouts  4.72 us

profile of v1, /device:TPU:32, one launch (start us, length us, event | category | flops | bytes accessed | tf_op | source)
XLA Modules:
  0.0 111.5 jit_solution(2322604759183163649)
XLA Ops:
  0.6 106.2 %shard_map.84 = (bf16[3,1024,256]{2,1,0:T(8,128)(2,1)}, f32[512,256]{1,0:T(8,128)}, f32[16,128]{1,0:T(8,128)}, f32[3,7,256]{2,1,0:T(8,128)}) custom-call(bf16[3,1024,256]{2,1,0:T(8,128)(2,1)} %proj.1, f32[3,7,256]{2,1,0:T(8,128)} %ff.1, bf16[16,128]{1,0:T(8,128)(2,1)} %lf.1, bf16[512,4096]{1,0:T(8,128)(2,1)} %w_hbm.1, bf16[1024,512]{1,0:T(8,128)(2,1)} %go_hbm.1), custom_call_target="tpu_custom_call" | custom-call | flops 8999999488 | bytes 20000000 | tf_op jit(solution)/shard_map/pallas_call | solution.py:518
  106.8 0.0 copy-start
  106.8 0.0 copy-start.2
  106.8 0.0 copy-start.1
  106.8 2.7 %copy.13 = bf16[3,1024,256]{2,1,0:T(8,128)(2,1)} copy(bf16[3,1024,256]{2,1,0:T(8,128)(2,1)} %get-tuple-element.8) | data formatting | bytes 3145728
  109.5 0.0 copy-done
  109.5 0.8 copy.14
  110.3 0.0 copy-done.2
  110.3 0.6 copy.15
  110.9 0.0 copy-done.1
  110.9 0.6 copy.16
Async XLA Ops:
  106.8 2.7 %copy-start = (f32[512,256]{1,0:T(8,128)S(1)}, f32[512,256]{1,0:T(8,128)}, u32[]{:S(2)}) copy-start(f32[512,256]{1,0:T(8,128)} %get-tuple-element.9) | copy-start | bytes 1572868
  106.8 3.5 %copy-start.2 = (f32[16,128]{1,0:T(8,128)S(1)}, f32[16,128]{1,0:T(8,128)}, u32[]{:S(2)}) copy-start(f32[16,128]{1,0:T(8,128)} %get-tuple-element.10) | copy-start | bytes 24580
  106.8 4.1 %copy-start.1 = (f32[3,7,256]{2,1,0:T(8,128)S(1)}, f32[3,7,256]{2,1,0:T(8,128)}, u32[]{:S(2)}) copy-start(f32[3,7,256]{2,1,0:T(8,128)} %get-tuple-element.11) | copy-start | bytes 64516

commit v2 on v1

--- a/solution.py
+++ b/solution.py
@@ -27,7 +27,10 @@
 RIM = 16
 ORDER = (0, 2, 1, 3)
 UNITS = 2 * PARTS
-COPIES = 160
+COPIES = 176
+PIECES = ((0, 0), (0, 1), (1, 0), (1, 1), (2, 0), (3, 0), (2, 1), (3, 1))
+HALF = TOK // 2
+UNROLL = 4
 
 
 def dot(a, b, dims):
@@ -36,7 +39,7 @@
 
 def kernel(
     grad_scale,
-    proj,
+    proj_hbm,
     ff,
     lf,
     w_hbm,
@@ -45,6 +48,7 @@
     gw_out,
     gl_out,
     gf_out,
+    proj,
     projx,
     feat,
     kvx,
@@ -67,9 +71,11 @@
     rim_in,
     rim_out,
     rim_back,
+    lagt,
     red,
-    redx,
-    redz,
+    redr,
+    redt,
+    redo,
     ssem,
     rsem,
     lsem,
@@ -84,6 +90,9 @@
     def at_z(k):
         return (((z + k) % Z) * 2 + xh, r, q)
 
+    def at_s(k):
+        return ((s + k) % seqs, r, q)
+
     def at_y(k):
         return (s, ((y + k) % Y) * 2 + core, q)
 
@@ -95,7 +104,6 @@
     column = (s, r, 1 - q)
     after = ((s + 1) % seqs, r, q)
     behind = ((s + seqs - 1) % seqs, r, q)
-    diagonal = (((z + 2 * xh - 1 + Z) % Z) * 2 + 1 - xh, r, q)
 
     used = [0]
     sent = []
@@ -125,16 +133,12 @@
             device_id_type=MESH,
         ).wait_recv()
 
-    w_loads = []
-    for p in range(PARTS):
-        for blk in range(2 * Y):
-            copy = pltpu.make_async_copy(
-                w_hbm.at[:, pl.ds(512 * blk + LANES * ORDER[p], LANES)],
-                wv.at[p, :, pl.ds(LANES * blk, LANES)],
-                lsem.at[p * 9 + blk],
-            )
-            copy.start()
-            w_loads.append(copy)
+    barrier = pltpu.get_barrier_semaphore()
+    partners = [at_s(k) for k in range(1, seqs)] + [at_y(1), at_y(Y - 1), sibling, column]
+    for device in partners:
+        pl.semaphore_signal(barrier, inc=1, device_id=device, device_id_type=MESH)
+    proj_load = pltpu.make_async_copy(proj_hbm, proj, lsem.at[9 * PARTS])
+    proj_load.start()
     own_loads = []
     for p in range(PARTS):
         copy = pltpu.make_async_copy(
@@ -142,44 +146,6 @@
         )
         copy.start()
         own_loads.append(copy)
-
-    barrier = pltpu.get_barrier_semaphore()
-    partners = [at_z(k) for k in range(1, Z)] + [at_y(1), at_y(-1 + Y), sibling, across, column, diagonal]
-    for device in partners:
-        pl.semaphore_signal(barrier, inc=1, device_id=device, device_id_type=MESH)
-    pl.semaphore_wait(barrier, len(partners))
-
-    ids = {}
-
-    def gather_direct(p):
-        src = go_hbm.at[:, pl.ds(LANES * ORDER[p], LANES)]
-        ids[p, 0] = push(src, gath.at[p, r], at_y(1))
-        ids[p, 1] = push(src, gath.at[p, r], at_y(Y - 1))
-        ids[p, 2] = push(src, gath.at[p, r], sibling)
-
-    half = pl.ds(0, TOK // 2), pl.ds(TOK // 2, TOK // 2)
-
-    def gather_forward(p):
-        low, high = row_y(Y - 1, core), row_y(1, core)
-        arrived(ids[p, 0], gath.at[p, low])
-        ids[p, 3] = push(gath.at[p, low, half[0]], gath.at[p, low, half[0]], at_y(1))
-        ids[p, 5] = push(gath.at[p, low], gath.at[p, low], sibling)
-        arrived(ids[p, 1], gath.at[p, high])
-        ids[p, 4] = push(gath.at[p, high, half[1]], gath.at[p, high, half[1]], at_y(Y - 1))
-        ids[p, 6] = push(gath.at[p, high], gath.at[p, high], sibling)
-
-    def gather_finish(p):
-        far = row_y(2, core)
-        arrived(ids[p, 3], gath.at[p, far, half[0]])
-        arrived(ids[p, 4], gath.at[p, far, half[1]])
-        ids[p, 7] = push(gath.at[p, far], gath.at[p, far], sibling)
-        own_loads[p].wait()
-        for idx, k in ((2, 0), (5, Y - 1), (6, 1), (7, 2)):
-            arrived(ids[p, idx], gath.at[p, row_y(k, 1 - core)])
-
-    gather_direct(0)
-    rim_id = push(proj.at[:, pl.ds(TOK - RIM, RIM), :], rim_in, after)
-    gather_direct(1)
 
     taps32 = lf[...].astype(F32)
     base = jnp.broadcast_to(taps32[:, None, :], (GROUPS, 8, LANES)).reshape(GROUPS * 8, LANES)
@@ -198,6 +164,61 @@
         toep[:, pl.ds(16 * a, 16), :] = jnp.where(later, both, 0.0).astype(BF16)
         toep[:, pl.ds(LANES + 16 * a, 16), :] = jnp.where(later, 0.0, both).astype(BF16)
 
+    pl.semaphore_wait(barrier, len(partners))
+
+    ids = {}
+
+    def tokens(hf, quarter=None):
+        if quarter is None:
+            return pl.ds(HALF * hf, HALF)
+        return pl.ds(HALF * hf + HALF // 2 * quarter, HALF // 2)
+
+    def direct(i):
+        p, hf = PIECES[i]
+        src = go_hbm.at[tokens(hf), pl.ds(LANES * ORDER[p], LANES)]
+        dst = gath.at[p, r, tokens(hf)]
+        ids[i, 0] = push(src, dst, at_y(1))
+        ids[i, 1] = push(src, dst, at_y(Y - 1))
+        ids[i, 2] = push(src, dst, sibling)
+
+    def forward(i):
+        p, hf = PIECES[i]
+        for way, k, there in ((0, Y - 1, 1), (1, 1, Y - 1)):
+            slot = row_y(k, core)
+            arrived(ids[i, way], gath.at[p, slot, tokens(hf)])
+            src = gath.at[p, slot, tokens(hf, way)]
+            ids[i, 3 + way] = push(src, src, at_y(there))
+            src = gath.at[p, slot, tokens(hf)]
+            ids[i, 5 + way] = push(src, src, sibling)
+
+    def finish(i):
+        p, hf = PIECES[i]
+        far = row_y(2, core)
+        for way in range(2):
+            arrived(ids[i, 3 + way], gath.at[p, far, tokens(hf, way)])
+        src = gath.at[p, far, tokens(hf)]
+        ids[i, 7] = push(src, src, sibling)
+        if hf == 0:
+            own_loads[p].wait()
+        for idx, k in ((2, 0), (5, Y - 1), (6, 1), (7, 2)):
+            arrived(ids[i, idx], gath.at[p, row_y(k, 1 - core), tokens(hf)])
+
+    direct(0)
+    proj_load.wait()
+    rim_id = push(proj.at[:, pl.ds(TOK - RIM, RIM), :], rim_in, after)
+    direct(1)
+    direct(2)
+    w_loads = []
+    for p in range(PARTS):
+        for blk in range(2 * Y):
+            copy = pltpu.make_async_copy(
+                w_hbm.at[:, pl.ds(512 * blk + LANES * ORDER[p], LANES)],
+                wv.at[p, :, pl.ds(LANES * blk, LANES)],
+                lsem.at[p * 9 + blk],
+            )
+            copy.start()
+            w_loads.append(copy)
+
     def widen(b, carry):
         rows = pl.ds(pl.multiple_of(b * LANES, LANES), LANES)
         dest = pl.ds(pl.multiple_of(b * LANES + RIM, RIM), LANES)
@@ -241,16 +262,16 @@
             projx[a, h, pl.ds(0, RIM), :] = before[:, LANES * h : LANES * h + LANES]
     featurize(0)
 
-    gather_forward(0)
-    gather_direct(2)
+    forward(0)
+    direct(3)
 
     arrived(hist_id, kvx.at[:, pl.ds(0, LANES)])
     past = kvx[:, pl.ds(0, LANES)]
     kvx[:, pl.ds(0, LANES)] = jnp.where(s == 0, jnp.zeros_like(past), past)
 
-    def stacked(ref, rows, first):
+    def stacked(ref, rows, first, count=BLOCKS):
         return jnp.concatenate(
-            [ref[rows, pl.ds(LANES * (b + first), LANES)] for b in range(BLOCKS)], axis=0
+            [ref[rows, pl.ds(LANES * (b + first), LANES)] for b in range(count)], axis=0
         )
 
     def convolve(g, carry):
@@ -266,7 +287,7 @@
 
     mix_ids = []
     for h in range(2):
-        lax.fori_loop(h * GROUPS // 2, (h + 1) * GROUPS // 2, convolve, 0)
+        lax.fori_loop(h * GROUPS // 2, (h + 1) * GROUPS // 2, convolve, 0, unroll=UNROLL)
         chans = pl.ds(LANES * h, LANES)
         mix_ids.append((push(mix.at[q, chans], mix.at[q, chans], column), chans))
 
@@ -316,19 +337,20 @@
         xs[pair] = gwacc[2 * pair + 1 - xh].astype(BF16)
         xids.append(push(xs.at[pair], xr.at[pair], across))
 
-    def tick(t):
-        if t < UNITS:
-            partial_weight(t)
-            hop(t, 4)
-        for lag in (1, 2, 3):
-            if 0 <= t - lag < UNITS:
-                hop(t - lag, 4 - lag)
-        if 0 <= t - 4 < UNITS:
-            final_sum(t - 4)
-            if t - 4 == 3:
-                exchange(0)
-            if t - 4 == 7:
-                exchange(1)
+    def weight(p):
+        for n in (2 * p, 2 * p + 1):
+            partial_weight(n)
+            hop(n, 4)
+
+    def hops(p, k):
+        for n in (2 * p, 2 * p + 1):
+            hop(n, k)
+
+    def finals(p):
+        for n in (2 * p, 2 * p + 1):
+            final_sum(n)
+        if p % 2 == 1:
+            exchange(p // 2)
 
     def mix_tile(p, hh, j):
         trows = pl.ds(pl.multiple_of(j * CH, CH), CH)
@@ -336,7 +358,9 @@
         rhs = jnp.concatenate([gath[p, i, trows, :] for i in range(2 * Y)], axis=1)
         return dot(wv[p, crows, :], rhs, NT)
 
-    def partial_mix(p):
+    def partial_mix(i):
+        p, hf = PIECES[i]
+
         def tile(j, carry):
             for hh in range(2):
                 value = mix_tile(p, hh, j)
@@ -346,98 +370,155 @@
                     pm[j, hh] += value
             return carry
 
-        lax.fori_loop(0, TOK // CH, tile, 0)
-
-    gather_forward(1)
-    gather_direct(3)
+        lax.fori_loop(2 * hf, 2 * hf + 2, tile, 0)
+
+    gm_ids = {}
+
+    def last_mix(hf):
+        for j in (2 * hf, 2 * hf + 1):
+            gms[j] = (pm[j, 1 - q] + mix_tile(PARTS - 1, 1 - q, j)).astype(BF16)
+            gm_ids[j] = push(gms.at[j], gmr.at[j], column)
+
+    def own_mix(hf):
+        for j in (2 * hf, 2 * hf + 1):
+            pm[j, q] += mix_tile(PARTS - 1, q, j)
+
+    future = []
+
+    def cotangents(hf):
+        for j in (2 * hf, 2 * hf + 1):
+            arrived(gm_ids[j], gmr.at[j])
+            cols = pl.ds(CH * j, CH)
+            cot = (pm[j, q] + gmr[j].astype(F32)).astype(BF16).astype(F32)
+            gcx[:, cols] = (cot * feat[0, :, cols]).astype(BF16)
+            if j == 0:
+                future.append(push(gcx.at[:, pl.ds(0, LANES)], gcx.at[:, pl.ds(TOK, LANES)], behind))
+            grad = (cot * conv[:, cols]).astype(BF16).astype(F32)
+            for h in range(2):
+                gtok[0, h, cols, :] = grad[LANES * h : LANES * h + LANES].T
+
+    lane = lax.broadcasted_iota(jnp.int32, (LANES, LANES), 1)
+    row = lax.broadcasted_iota(jnp.int32, (LANES, LANES), 0)
+
+    def lag_sums():
+        def lags(g, carry):
+            rows = pl.ds(pl.multiple_of(g * GS, GS), GS)
+            cot = stacked(gcx, rows, 0)
+            windows = jnp.concatenate([stacked(kvx, rows, 0), stacked(kvx, rows, 1)], axis=1)
+            both = dot(cot, windows, TN)
+            table = jnp.where(lane > row, both[:, :LANES], both[:, LANES:])
+            height = LANES // 2
+            while height >= 8:
+                table = table[:height] + pltpu.roll(table[height:], LANES - height, 1)
+                height //= 2
+            lagt[pl.ds(pl.multiple_of(g * 8, 8), 8), :] = table
+            return carry
+
+        lax.fori_loop(0, GROUPS, lags, 0, unroll=UNROLL)
+        table = lagt[...]
+        for bit in (1, 2, 4):
+            table = jnp.where((sub // bit) % 2 == 1, pltpu.roll(table, LANES - bit, 1), table)
+        sums = jnp.sum(table.reshape(GROUPS, 8, LANES), axis=1)
+        turned = ((lane + row) % LANES == 0).astype(F32)
+        sums = lax.dot_general(
+            sums, turned, NN, precision=lax.Precision.HIGHEST, preferred_element_type=F32
+        )
+        for c in range(4):
+            red[c, pl.ds(0, 4), :] = sums[4 * c : 4 * c + 4]
+
+    def deconvolve(first, count):
+        def group(g, carry):
+            rows = pl.ds(pl.multiple_of(g * GS, GS), GS)
+            windows = jnp.concatenate(
+                [stacked(gcx, rows, first, count), stacked(gcx, rows, first + 1, count)], axis=1
+            )
+            band = jnp.concatenate(
+                [toep[g, pl.ds(LANES, LANES), :], toep[g, pl.ds(0, LANES), :]], axis=1
+            )
+            result = dot(windows, band, NT)
+            for b in range(count):
+                cols = pl.ds(LANES * (first + b), LANES)
+                piece = result[GS * b : GS * b + GS]
+                gback[0, rows, cols] = (piece * feat[2, rows, cols]).astype(BF16).astype(F32)
+                gback[1, rows, cols] = (piece * feat[1, rows, cols]).astype(BF16).astype(F32)
+            return carry
+
+        lax.fori_loop(0, GROUPS, group, 0, unroll=UNROLL)
+
+        def turn(b, carry):
+            cols = pl.ds(pl.multiple_of(b * LANES, LANES), LANES)
+            for a in range(2):
+                for h in range(2):
+                    gtok[a + 1, h, cols, :] = gback[a, pl.ds(LANES * h, LANES), cols].T
+            return carry
+
+        lax.fori_loop(first, first + count, turn, 0)
+
+    red[...] = jnp.zeros_like(red)
     for copy in w_loads:
         copy.wait()
-    for p in range(PARTS - 1):
-        gather_finish(p)
-        tick(2 * p)
-        gather_forward(p + 2) if p + 2 < PARTS else None
-        partial_mix(p)
-        if p == 0:
-            for idx, chans in mix_ids:
-                arrived(idx, mix.at[1 - q, chans])
-        tick(2 * p + 1)
-
-    last = PARTS - 1
-    gather_finish(last)
-    gm_ids = []
-    for j in range(TOK // CH):
-        gms[j] = (pm[j, 1 - q] + mix_tile(last, 1 - q, j)).astype(BF16)
-        gm_ids.append(push(gms.at[j], gmr.at[j], column))
-    tick(6)
-    for j in range(TOK // CH):
-        pm[j, q] += mix_tile(last, q, j)
-    tick(7)
-
-    for j in range(TOK // CH):
-        arrived(gm_ids[j], gmr.at[j])
-        cols = pl.ds(CH * j, CH)
-        cot = (pm[j, q] + gmr[j].astype(F32)).astype(BF16).astype(F32)
-        gcx[:, cols] = (cot * feat[0, :, cols]).astype(BF16)
-        gback[0, :, cols] = (cot * conv[:, cols]).astype(BF16).astype(F32)
-        if j == 0:
-            future_id = push(gcx.at[:, pl.ds(0, LANES)], gcx.at[:, pl.ds(TOK, LANES)], behind)
-    tick(8)
-
-    lane = lax.broadcasted_iota(jnp.int32, (LANES, LANES), 1)
-    row = lax.broadcasted_iota(jnp.int32, (LANES, LANES), 0)
-
-    def lags(g, carry):
-        rows = pl.ds(pl.multiple_of(g * GS, GS), GS)
-        cot = stacked(gcx, rows, 0)
-        upper = dot(stacked(kvx, rows, 0), cot, TN)
-        lower = dot(stacked(kvx, rows, 1), cot, TN)
-        table = jnp.where(lane < row, upper, lower)
-        height = LANES // 2
-        while height >= 8:
-            table = table[:height] + pltpu.roll(table[height:], LANES - height, 1)
-            height //= 2
-        redx[1, pl.ds(pl.multiple_of(g * 8, 8), 8), :] = table
-        return carry
-
-    lax.fori_loop(0, GROUPS, lags, 0)
-    table = redx[1]
-    for bit in (1, 2, 4):
-        table = jnp.where((sub // bit) % 2 == 1, pltpu.roll(table, LANES - bit, 1), table)
-    red[pl.ds(0, GROUPS), :] = jnp.sum(table.reshape(GROUPS, 8, LANES), axis=1)
-    tick(9)
-
-    arrived(future_id, gcx.at[:, pl.ds(TOK, LANES)])
-    coming = gcx[:, pl.ds(TOK, LANES)]
-    gcx[:, pl.ds(TOK, LANES)] = jnp.where(s == seqs - 1, jnp.zeros_like(coming), coming)
-
-    def deconvolve(g, carry):
-        rows = pl.ds(pl.multiple_of(g * GS, GS), GS)
-        windows = jnp.concatenate([stacked(gcx, rows, 0), stacked(gcx, rows, 1)], axis=1)
-        band = jnp.concatenate([toep[g, pl.ds(LANES, LANES), :], toep[g, pl.ds(0, LANES), :]], axis=1)
-        result = dot(windows, band, NT)
-        for b in range(BLOCKS):
-            cols = pl.ds(LANES * b, LANES)
-            piece = result[GS * b : GS * b + GS]
-            gback[1, rows, cols] = (piece * feat[2, rows, cols]).astype(BF16).astype(F32)
-            gback[2, rows, cols] = (piece * feat[1, rows, cols]).astype(BF16).astype(F32)
-        return carry
-
-    lax.fori_loop(0, GROUPS, deconvolve, 0)
-    tick(10)
-
-    def turn(b, carry):
-        cols = pl.ds(pl.multiple_of(b * LANES, LANES), LANES)
-        for a in range(3):
-            for h in range(2):
-                gtok[a, h, cols, :] = gback[a, pl.ds(LANES * h, LANES), cols].T
-        return carry
-
-    lax.fori_loop(0, BLOCKS, turn, 0)
+    forward(1)
+    direct(4)
+    finish(0)
+    partial_mix(0)
+    forward(2)
+    direct(5)
+    finish(1)
+    partial_mix(1)
+    forward(3)
+    direct(6)
+    for idx, chans in mix_ids:
+        arrived(idx, mix.at[1 - q, chans])
+    weight(0)
+    finish(2)
+    partial_mix(2)
+    forward(4)
+    direct(7)
+    hops(0, 3)
+    finish(3)
+    partial_mix(3)
+    forward(5)
+    weight(1)
+    hops(0, 2)
+    finish(4)
+    partial_mix(4)
+    forward(6)
+    hops(1, 3)
+    finish(5)
+    last_mix(0)
+    own_mix(0)
+    forward(7)
+    hops(0, 1)
+    finish(6)
+    partial_mix(6)
+    weight(2)
+    hops(1, 2)
+    finish(7)
+    last_mix(1)
+    weight(3)
+    own_mix(1)
+    cotangents(0)
+    hops(2, 3)
+    finals(0)
+    hops(1, 1)
+    early = 3
+    deconvolve(0, early)
     for a in range(3):
         for h in range(2):
             rim_out[a, :, pl.ds(LANES * h, LANES)] = gtok[a, h, pl.ds(0, RIM), :].astype(BF16)
     back_id = push(rim_out, rim_back, behind)
-    tick(11)
+    hops(3, 3)
+    hops(2, 2)
+    finals(1)
+    hops(3, 2)
+    cotangents(1)
+    hops(2, 1)
+    lag_sums()
+    arrived(future[0], gcx.at[:, pl.ds(TOK, LANES)])
+    coming = gcx[:, pl.ds(TOK, LANES)]
+    gcx[:, pl.ds(TOK, LANES)] = jnp.where(s == seqs - 1, jnp.zeros_like(coming), coming)
+    hops(3, 1)
+    deconvolve(early, BLOCKS - early)
 
     span = 64
 
@@ -452,14 +533,14 @@
             return tuple(out)
 
         sums = lax.fori_loop(0, TOK // span, body, tuple(jnp.zeros((8, LANES), F32) for _ in range(TAPS)))
-        rows = [jnp.sum(x, axis=0, keepdims=True) for x in sums] + [jnp.zeros((1, LANES), F32)]
-        red[pl.ds(GROUPS + 8 * (2 * a + h), 8), :] = jnp.concatenate(rows, axis=0)
+        for i in range(TAPS):
+            at = 4 + 2 * (2 * a + h) + i // 4
+            red[at, pl.ds(i % 4, 1), :] = jnp.sum(sums[i], axis=0, keepdims=True)
 
     for a in range(3):
         for h in range(2):
             tap_sums(a, h)
-    width = GROUPS + 48
-    red_id = push(red, redx.at[0, pl.ds(0, width), :], across)
+    red_ids = [push(red.at[(s + k) % seqs], redr.at[k], at_s(k)) for k in range(1, seqs)]
 
     def taps_back(a, h, first, count):
         chans = pl.ds(LANES * h, LANES)
@@ -474,11 +555,17 @@
 
         lax.fori_loop(first, first + count, body, 0)
 
+    finals(2)
     for h in range(2):
         taps_back(0, h, 0, TOK // span - 1)
-    arrived(red_id, redx.at[0, pl.ds(0, width), :])
-    redz[0] = red[...] + redx[0, pl.ds(0, width), :]
-    z_ids = [push(redz.at[0], redz.at[k], at_z(k)) for k in range(1, Z)]
+    finals(3)
+    total = red[s]
+    for k in range(1, seqs):
+        arrived(red_ids[k - 1], redr.at[k])
+        total = total + redr[k]
+    redt[...] = total * grad_scale
+    redo[s] = redt[...]
+    all_ids = [push(redt, redo.at[s], at_s(k)) for k in range(1, seqs)]
     for a in (1, 2):
         for h in range(2):
             taps_back(a, h, 0, TOK // span - 1)
@@ -496,17 +583,15 @@
                 gwacc[2 * pair + xh, hh] + xr[pair, hh].astype(F32)
             ) * grad_scale
 
-    for k in range(1, Z):
-        arrived(z_ids[k - 1], redz.at[k])
-    total = redz[0]
-    for k in range(1, Z):
-        total = total + redz[k]
-    total = total * grad_scale
-    gl_out[...] = total[:GROUPS]
+    for k in range(1, seqs):
+        arrived(all_ids[k - 1], redo.at[(s + seqs - k) % seqs])
+    for c in range(4):
+        gl_out[pl.ds(4 * c, 4), :] = redo[c, pl.ds(0, 4), :]
     for a in range(3):
         for h in range(2):
-            at = GROUPS + 8 * (2 * a + h)
-            gf_out[a, :, pl.ds(LANES * h, LANES)] = total[at : at + TAPS]
+            at = 4 + 2 * (2 * a + h)
+            gf_out[a, pl.ds(0, 4), pl.ds(LANES * h, LANES)] = redo[at, pl.ds(0, 4), :]
+            gf_out[a, pl.ds(4, 3), pl.ds(LANES * h, LANES)] = redo[at + 1, pl.ds(0, 3), :]
     for copy in sent:
         copy.wait_send()
 
@@ -518,14 +603,15 @@
     return pl.pallas_call(
         functools.partial(kernel, grad_scale),
         out_shape=(
-            jax.ShapeDtypeStruct((3, TOK, CH), BF16),
-            jax.ShapeDtypeStruct((2 * CH, 2 * LANES), F32),
-            jax.ShapeDtypeStruct((GROUPS, LANES), F32),
-            jax.ShapeDtypeStruct((3, TAPS, CH), F32),
+            pltpu.VMEM((3, TOK, CH), BF16),
+            pltpu.VMEM((2 * CH, 2 * LANES), F32),
+            pltpu.VMEM((GROUPS, LANES), F32),
+            pltpu.VMEM((3, TAPS, CH), F32),
         ),
-        in_specs=[vmem, vmem, vmem, anywhere, anywhere],
+        in_specs=[anywhere, vmem, vmem, anywhere, anywhere],
         out_specs=(vmem, vmem, vmem, vmem),
         scratch_shapes=[
+            pltpu.VMEM((3, TOK, CH), BF16),
             pltpu.VMEM((3, 2, TOK + RIM, LANES), F32),
             pltpu.VMEM((3, CH, TOK), F32),
             pltpu.VMEM((CH, TOK + LANES), BF16),
@@ -543,20 +629,22 @@
             pltpu.VMEM((TOK // CH, CH, CH), BF16),
             pltpu.VMEM((TOK // CH, CH, CH), BF16),
             pltpu.VMEM((CH, TOK + LANES), BF16),
-            pltpu.VMEM((3, CH, TOK), F32),
+            pltpu.VMEM((2, CH, TOK), F32),
             pltpu.VMEM((3, 2, TOK + RIM, LANES), F32),
             pltpu.VMEM((3, RIM, CH), BF16),
             pltpu.VMEM((3, RIM, CH), BF16),
             pltpu.VMEM((3, RIM, CH), BF16),
-            pltpu.VMEM((GROUPS + 48, LANES), F32),
-            pltpu.VMEM((2, 8 * GROUPS, LANES), F32),
-            pltpu.VMEM((Z, GROUPS + 48, LANES), F32),
+            pltpu.VMEM((8 * GROUPS, LANES), F32),
+            pltpu.VMEM((2 * Z, 8, LANES), F32),
+            pltpu.VMEM((2 * Z, 8, LANES), F32),
+            pltpu.VMEM((8, LANES), F32),
+            pltpu.VMEM((2 * Z, 8, LANES), F32),
             pltpu.SemaphoreType.DMA((COPIES,)),
             pltpu.SemaphoreType.DMA((COPIES,)),
-            pltpu.SemaphoreType.DMA((9 * PARTS,)),
+            pltpu.SemaphoreType.DMA((9 * PARTS + 1,)),
         ],
         compiler_params=pltpu.CompilerParams(
-            collective_id=0, has_side_effects=True, vmem_limit_bytes=60 * 1024 * 1024
+            collective_id=0, has_side_effects=True, vmem_limit_bytes=56 * 1024 * 1024
         ),
         cost_estimate=pl.CostEstimate(
             flops=9_000_000_000, bytes_accessed=20_000_000, transcendentals=0

time: 112 us -> 99.3 us (0.89)
  Pallas kernels: 106 us -> 95.4 us
  local copies, waits for them, and re-layouts: 4.72 us -> 3.14 us
    pallas_call x1, Pallas kernels: 106 us -> 95.4 us  [on_device(): pl.pallas_call(functools.partial(kernel, grad_scale), out_shape=(pltpu.VM...]
    unnamed x10 -> x4, local copies, waits for them, and re-layouts: 4.72 us -> 3.14 us
where the time goes in v2:
time: 99.3 us; the launch traced here: 99.2 us
  Pallas kernels  95.4 us (96%)
  local copies, waits for them, and re-layouts  3.14 us (3%)
    pallas_call x1, Pallas kernels, on_device(): pl.pallas_call(functools.partial(kernel, grad_scale), out_shape=(pltpu.VM...  95.4 us
    unnamed x4, local copies, waits for them, and re-layouts  3.14 us

profile of v2, /device:TPU:32, one launch (start us, length us, event | category | flops | bytes accessed | tf_op | source)
XLA Modules:
  0.0 99.2 jit_solution(13746452633956694937)
XLA Ops:
  0.6 95.4 %shard_map.84 = (bf16[3,1024,256]{2,1,0:T(8,128)(2,1)S(1)}, f32[512,256]{1,0:T(8,128)S(1)}, f32[16,128]{1,0:T(8,128)S(1)}, f32[3,7,256]{2,1,0:T(8,128)S(1)}) custom-call(bf16[3,1024,256]{2,1,0:T(8,128)(2,1)} %proj_hbm.1, f32[3,7,256]{2,1,0:T(8,128)} %ff.1, bf16[16,128]{1,0:T(8,128)(2,1)} %lf.1, bf16[512,4096]{1,0:T(8,128)(2,1)} %w_hbm.1, ...), custom_call_target="tpu_custom_call" | custom-call | flops 8999999488 | bytes 20000000 | tf_op jit(solution)/shard_map/pallas_call | solution.py:603
  96.0 1.1 %copy.13 = bf16[3,1024,256]{2,1,0:T(8,128)(2,1)} copy(bf16[3,1024,256]{2,1,0:T(8,128)(2,1)S(1)} %get-tuple-element.4) | data formatting | bytes 3145728
  97.2 0.6 copy.15
  97.8 0.6 copy.16
  98.4 0.8 copy.14

commit v3 on v2

--- a/solution.py
+++ b/solution.py
@@ -207,7 +207,6 @@
     proj_load.wait()
     rim_id = push(proj.at[:, pl.ds(TOK - RIM, RIM), :], rim_in, after)
     direct(1)
-    direct(2)
     w_loads = []
     for p in range(PARTS):
         for blk in range(2 * Y):
@@ -263,7 +262,7 @@
     featurize(0)
 
     forward(0)
-    direct(3)
+    direct(2)
 
     arrived(hist_id, kvx.at[:, pl.ds(0, LANES)])
     past = kvx[:, pl.ds(0, LANES)]
@@ -337,10 +336,9 @@
         xs[pair] = gwacc[2 * pair + 1 - xh].astype(BF16)
         xids.append(push(xs.at[pair], xr.at[pair], across))
 
-    def weight(p):
-        for n in (2 * p, 2 * p + 1):
-            partial_weight(n)
-            hop(n, 4)
+    def weight(n):
+        partial_weight(n)
+        hop(n, 4)
 
     def hops(p, k):
         for n in (2 * p, 2 * p + 1):
@@ -458,29 +456,34 @@
     for copy in w_loads:
         copy.wait()
     forward(1)
-    direct(4)
+    direct(3)
     finish(0)
     partial_mix(0)
     forward(2)
-    direct(5)
+    direct(4)
     finish(1)
+    weight(0)
     partial_mix(1)
     forward(3)
-    direct(6)
+    direct(5)
     for idx, chans in mix_ids:
         arrived(idx, mix.at[1 - q, chans])
-    weight(0)
+    weight(1)
     finish(2)
     partial_mix(2)
     forward(4)
+    direct(6)
+    hop(0, 3)
+    finish(3)
+    weight(2)
+    hop(1, 3)
+    forward(5)
     direct(7)
-    hops(0, 3)
-    finish(3)
+    weight(3)
+    hop(0, 2)
     partial_mix(3)
-    forward(5)
-    weight(1)
-    hops(0, 2)
     finish(4)
+    hop(1, 2)
     partial_mix(4)
     forward(6)
     hops(1, 3)
@@ -488,19 +491,21 @@
     last_mix(0)
     own_mix(0)
     forward(7)
+    finish(6)
     hops(0, 1)
-    finish(6)
+    hops(1, 2)
+    weight(4)
+    weight(5)
     partial_mix(6)
-    weight(2)
-    hops(1, 2)
     finish(7)
     last_mix(1)
-    weight(3)
+    weight(6)
+    weight(7)
     own_mix(1)
-    cotangents(0)
+    hops(1, 1)
     hops(2, 3)
     finals(0)
-    hops(1, 1)
+    cotangents(0)
     early = 3
     deconvolve(0, early)
     for a in range(3):
@@ -510,14 +515,13 @@
     hops(3, 3)
     hops(2, 2)
     finals(1)
+    cotangents(1)
+    lag_sums()
     hops(3, 2)
-    cotangents(1)
     hops(2, 1)
-    lag_sums()
     arrived(future[0], gcx.at[:, pl.ds(TOK, LANES)])
     coming = gcx[:, pl.ds(TOK, LANES)]
     gcx[:, pl.ds(TOK, LANES)] = jnp.where(s == seqs - 1, jnp.zeros_like(coming), coming)
-    hops(3, 1)
     deconvolve(early, BLOCKS - early)
 
     span = 64
@@ -555,10 +559,10 @@
 
         lax.fori_loop(first, first + count, body, 0)
 
+    hops(3, 1)
     finals(2)
     for h in range(2):
         taps_back(0, h, 0, TOK // span - 1)
-    finals(3)
     total = red[s]
     for k in range(1, seqs):
         arrived(red_ids[k - 1], redr.at[k])
@@ -566,6 +570,7 @@
     redt[...] = total * grad_scale
     redo[s] = redt[...]
     all_ids = [push(redt, redo.at[s], at_s(k)) for k in range(1, seqs)]
+    finals(3)
     for a in (1, 2):
         for h in range(2):
             taps_back(a, h, 0, TOK // span - 1)

time: 99.3 us -> 95.3 us (0.960)
  Pallas kernels: 95.4 us -> 91 us
    pallas_call x1, Pallas kernels: 95.4 us -> 91 us  [on_device(): pl.pallas_call(functools.partial(kernel, grad_scale), out_shape=(pltpu.VM...]
where the time goes in v3:
time: 95.3 us; the launch traced here: 94.7 us
  Pallas kernels  91 us (95%)
  local copies, waits for them, and re-layouts  3.14 us (3%)
    pallas_call x1, Pallas kernels, on_device(): pl.pallas_call(functools.partial(kernel, grad_scale), out_shape=(pltpu.VM...  91 us
    unnamed x4, local copies, waits for them, and re-layouts  3.14 us

profile of v3, /device:TPU:32, one launch (start us, length us, event | category | flops | bytes accessed | tf_op | source)
XLA Modules:
  0.0 94.7 jit_solution(15113773072128129494)
XLA Ops:
  0.6 91.0 %shard_map.84 = (bf16[3,1024,256]{2,1,0:T(8,128)(2,1)S(1)}, f32[512,256]{1,0:T(8,128)S(1)}, f32[16,128]{1,0:T(8,128)S(1)}, f32[3,7,256]{2,1,0:T(8,128)S(1)}) custom-call(bf16[3,1024,256]{2,1,0:T(8,128)(2,1)} %proj_hbm.1, f32[3,7,256]{2,1,0:T(8,128)} %ff.1, bf16[16,128]{1,0:T(8,128)(2,1)} %lf.1, bf16[512,4096]{1,0:T(8,128)(2,1)} %w_hbm.1, ...), custom_call_target="tpu_custom_call" | custom-call | flops 8999999488 | bytes 20000000 | tf_op jit(solution)/shard_map/pallas_call | solution.py:608
  91.6 1.1 %copy.13 = bf16[3,1024,256]{2,1,0:T(8,128)(2,1)} copy(bf16[3,1024,256]{2,1,0:T(8,128)(2,1)S(1)} %get-tuple-element.4) | data formatting | bytes 3145728
  92.7 0.6 copy.15
  93.3 0.6 copy.16
  94.0 0.8 copy.14

commit v4 on v3

--- a/solution.py
+++ b/solution.py
@@ -466,14 +466,14 @@
     partial_mix(1)
     forward(3)
     direct(5)
-    for idx, chans in mix_ids:
-        arrived(idx, mix.at[1 - q, chans])
-    weight(1)
     finish(2)
     partial_mix(2)
     forward(4)
     direct(6)
     hop(0, 3)
+    for idx, chans in mix_ids:
+        arrived(idx, mix.at[1 - q, chans])
+    weight(1)
     finish(3)
     weight(2)
     hop(1, 3)

time: 95.3 us -> 95.3 us (level)
  no operation moved by 1% of the time
where the time goes in v4:
time: 95.3 us; the launch traced here: 94.7 us
  Pallas kernels  91 us (95%)
  local copies, waits for them, and re-layouts  3.14 us (3%)
    pallas_call x1, Pallas kernels, on_device(): pl.pallas_call(functools.partial(kernel, grad_scale), out_shape=(pltpu.VM...  91 us
    unnamed x4, local copies, waits for them, and re-layouts  3.14 us

profile of v4, /device:TPU:32, one launch (start us, length us, event | category | flops | bytes accessed | tf_op | source)
XLA Modules:
  0.0 94.7 jit_solution(5596006868605553786)
XLA Ops:
  0.6 91.0 %shard_map.84 = (bf16[3,1024,256]{2,1,0:T(8,128)(2,1)S(1)}, f32[512,256]{1,0:T(8,128)S(1)}, f32[16,128]{1,0:T(8,128)S(1)}, f32[3,7,256]{2,1,0:T(8,128)S(1)}) custom-call(bf16[3,1024,256]{2,1,0:T(8,128)(2,1)} %proj_hbm.1, f32[3,7,256]{2,1,0:T(8,128)} %ff.1, bf16[16,128]{1,0:T(8,128)(2,1)} %lf.1, bf16[512,4096]{1,0:T(8,128)(2,1)} %w_hbm.1, ...), custom_call_target="tpu_custom_call" | custom-call | flops 8999999488 | bytes 20000000 | tf_op jit(solution)/shard_map/pallas_call | solution.py:608
  91.6 1.1 %copy.13 = bf16[3,1024,256]{2,1,0:T(8,128)(2,1)} copy(bf16[3,1024,256]{2,1,0:T(8,128)(2,1)S(1)} %get-tuple-element.4) | data formatting | bytes 3145728
  92.7 0.6 copy.15
  93.3 0.6 copy.16
  94.0 0.8 copy.14
